TPU v7x, 32 devices: a whole 2x2x4 slice. The times are simulated.
32 devices in a mesh: ctx: 16 (over z, y, core), head: 2 (over x).
Axes of the slice: x: 2, y: 2, z: 4, core: 2. Of those that a mesh axis runs over, the one named last changes fastest.
Arguments:
- response_input: bfloat16 [64, 8192], P(('ctx', 'head')), may hold values from -6 to 6
- response_queries: bfloat16 [64, 8192], P(('ctx', 'head')), may hold values from -12 to 12
- response_keys: bfloat16 [64, 8192], P(('ctx', 'head')), may hold values from -6 to 6
- response_values: bfloat16 [64, 8192], P(('ctx', 'head')), may hold values from -6 to 6
- prompt_keys: bfloat16 [24576, 8192], P('ctx', 'head'), may hold values from -6 to 6
- prompt_values: bfloat16 [24576, 8192], P('ctx', 'head'), may hold values from -6 to 6
- query_down_weight: bfloat16 [8192, 16], replicated, may hold values from -0.0625 to 0.0625
- query_up_weight: bfloat16 [16, 8192], replicated, may hold values from -1.5 to 1.5
- value_down_weight: bfloat16 [8192, 16], replicated, may hold values from -0.0625 to 0.0625
- value_up_weight: bfloat16 [16, 8192], replicated, may hold values from -1.5 to 1.5
- response_index: int32 [64], replicated, may hold values from 0 to 7, never falling along the last dimension, each value on 1 to 16 neighbouring positions
Outputs:
- out_adapted: bfloat16 [64, 8192], P(('ctx', 'head'))
- out_base: bfloat16 [64, 8192], P(('ctx', 'head'))
Inputs may be any that keep to these rules, and one draw needn't show every extreme that they name: `response_index`: never falls along the tokens; each response spans 1 to 16 tokens and one spans exactly 16.
All inputs are finite; a program needn't handle non-finite values.
Results may differ from a plain program's by a relative error of at most 0.0088.
Values may be sent and summed in bfloat16 or wider, within the bound.
A program may use at most 128 MiB of HBM per device.

v0:
```python
import jax
import jax.numpy as jnp
from jax import lax
from jax.sharding import PartitionSpec as P

HD = 128


def partial_block(
    start,
    queries_all,
    key_rows,
    value_rows,
    response_index,
    key_pos,
    key_seg,
    cache_rows,
    block_rows,
):
    scale = HD ** (-0.5)
    query_block = lax.dynamic_slice_in_dim(queries_all, start, block_rows, 0)
    scores = (
        jnp.einsum("qshd,khd->qshk", query_block, key_rows, preferred_element_type=jnp.float32)
        * scale
    )
    query_pos = start + jnp.arange(block_rows, dtype=jnp.int32)
    query_seg = lax.dynamic_slice_in_dim(response_index, start, block_rows, 0)
    stretch_ok = (key_pos[None, :] <= query_pos[:, None]) & (key_seg[None, :] == query_seg[:, None])
    visible = jnp.concatenate([jnp.ones((block_rows, cache_rows), bool), stretch_ok], 1)
    scores = jnp.where(visible[:, None, None, :], scores, -jnp.inf)
    row_max = jnp.max(scores, -1)
    probs = jnp.exp(scores - row_max[..., None]).astype(jnp.bfloat16)
    part_total = jnp.sum(probs.astype(jnp.float32), -1)
    part_out = jnp.einsum("qshk,kshd->qshd", probs, value_rows, preferred_element_type=jnp.float32)
    part_mean = (part_out / part_total[..., None]).astype(jnp.bfloat16)
    return (part_mean, part_total, row_max)


def local(
    response_input,
    response_queries,
    response_keys,
    response_values,
    prompt_keys,
    prompt_values,
    query_down_weight,
    query_up_weight,
    value_down_weight,
    value_up_weight,
    response_index,
):
    groups = lax.axis_size("head")
    group_width = response_queries.shape[1] // groups
    head_count = group_width // HD
    ctx_index = lax.axis_index("ctx")
    query_lowrank = jnp.dot(
        response_input, query_down_weight, preferred_element_type=jnp.float32
    ).astype(jnp.bfloat16)
    value_lowrank = jnp.dot(
        response_input, value_down_weight, preferred_element_type=jnp.float32
    ).astype(jnp.bfloat16)
    query_with_adapter = (
        response_queries.astype(jnp.float32)
        + jnp.dot(query_lowrank, query_up_weight, preferred_element_type=jnp.float32)
    ).astype(jnp.bfloat16)
    value_with_adapter = (
        response_values.astype(jnp.float32)
        + jnp.dot(value_lowrank, value_up_weight, preferred_element_type=jnp.float32)
    ).astype(jnp.bfloat16)
    heads_q, heads_k, stretch_values = (
        lax.all_to_all(
            jnp.stack([query_with_adapter, response_queries], 1),
            "head",
            split_axis=2,
            concat_axis=0,
            tiled=True,
        ),
        lax.all_to_all(response_keys[:, None, :], "head", split_axis=2, concat_axis=0, tiled=True),
        lax.all_to_all(
            jnp.stack([value_with_adapter, response_values], 1),
            "head",
            split_axis=2,
            concat_axis=0,
            tiled=True,
        ),
    )
    stretch_keys = heads_k[:, 0, :]
    queries_all = lax.all_gather(heads_q, "ctx", axis=0, tiled=True)
    shard_rows = stretch_keys.shape[0]
    cache_rows = prompt_keys.shape[0]
    query_count = queries_all.shape[0]
    queries_all = queries_all.reshape(query_count, 2, head_count, HD)
    key_rows = jnp.concatenate([prompt_keys, stretch_keys], 0).reshape(-1, head_count, HD)
    cache_pair = jnp.broadcast_to(prompt_values[:, None, :], (cache_rows, 2, group_width))
    value_rows = jnp.concatenate([cache_pair, stretch_values], 0).reshape(-1, 2, head_count, HD)
    stretch_start = ctx_index * shard_rows
    key_pos = stretch_start + jnp.arange(shard_rows, dtype=jnp.int32)
    key_seg = lax.dynamic_slice_in_dim(response_index, stretch_start, shard_rows, 0)
    block_rows = 128 if query_count % 128 == 0 else query_count

    def one_block(block_index):
        return partial_block(
            block_index * block_rows,
            queries_all,
            key_rows,
            value_rows,
            response_index,
            key_pos,
            key_seg,
            cache_rows,
            block_rows,
        )

    part_mean, part_total, part_max = lax.map(
        one_block, jnp.arange(query_count // block_rows, dtype=jnp.int32)
    )
    part_mean = part_mean.reshape(query_count, 2, group_width)
    part_total = part_total.reshape(query_count, 2, head_count)
    part_max = part_max.reshape(query_count, 2, head_count)
    out_parts = lax.all_to_all(part_mean[None], "ctx", split_axis=1, concat_axis=0, tiled=True)
    total_parts, max_parts = (
        lax.all_to_all(part_total[None], "ctx", split_axis=1, concat_axis=0, tiled=True),
        lax.all_to_all(part_max[None], "ctx", split_axis=1, concat_axis=0, tiled=True),
    )
    best = jnp.max(max_parts, 0)
    part_weight = total_parts * jnp.exp(max_parts - best[None])
    parts_count = out_parts.shape[0]
    weighted = jnp.sum(
        out_parts.reshape(parts_count, shard_rows, 2, head_count, HD).astype(jnp.float32)
        * part_weight[..., None],
        0,
    )
    totals = jnp.sum(part_weight, 0)
    result = (weighted / totals[..., None]).astype(jnp.bfloat16).reshape(shard_rows, 2, group_width)
    out_adapted, out_base = (
        lax.all_to_all(result[:, 0], "head", split_axis=0, concat_axis=1, tiled=True),
        lax.all_to_all(result[:, 1], "head", split_axis=0, concat_axis=1, tiled=True),
    )
    return (out_adapted, out_base)


def solution(mesh):
    placed = (
        P(("ctx", "head"), None),
        P(("ctx", "head"), None),
        P(("ctx", "head"), None),
        P(("ctx", "head"), None),
        P("ctx", "head"),
        P("ctx", "head"),
        P(),
        P(),
        P(),
        P(),
        P(),
    )
    return jax.shard_map(
        local,
        mesh=mesh,
        in_specs=placed,
        out_specs=(P(("ctx", "head"), None), P(("ctx", "head"), None)),
        check_vma=False,
    )
```

profile of v0, /device:TPU:0, one launch (start us, length us, event | category | flops | bytes accessed | tf_op | source)
XLA Modules:
  0.0 347.8 jit_solution(2086293497414106246)
XLA Ops:
  7.2 0.0 all-gather.2.cloned.1.call-start
  7.2 0.9 copy-done
  8.1 1.4 fusion.11
  9.5 0.9 pad_maximum_fusion.1
  10.4 6.9 %copy.138 = bf16[2,2,8192]{0,1,2:T(2,128)(2,1)} copy(bf16[2,2,8192]{2,0,1:T(2,128)(2,1)S(1)} %pad_maximum_fusion.1) | data formatting | bytes 131072 | tf_op jit(solution)/shard_map/stack | solution.py:72
  17.2 9.1 %reshape.97 = bf16[2,2,8192]{2,1,0:T(2,128)(2,1)S(1)} reshape(bf16[8192,2,2]{2,1,0:T(2,128)(2,1)} %bitcast.76) | data formatting | bytes 131072
  26.3 8.1 %all_to_all.119 = bf16[2,2,8192]{2,1,0:T(2,128)(2,1)S(1)} all-to-all(bf16[2,2,8192]{2,1,0:T(2,128)(2,1)S(1)} %reshape.97), channel_id=1, replica_groups=mesh['ctx'=16,'head'=2] {'head'}, dimensions={0} | all-to-all | bytes 131072 | tf_op jit(solution)/shard_map/all_to_all | solution.py:71
  34.4 10.3 %reshape.98 = bf16[8192,2,2]{2,1,0:T(2,128)(2,1)} reshape(bf16[2,2,8192]{2,1,0:T(2,128)(2,1)S(1)} %all_to_all.119) | data formatting | bytes 131072
  44.8 9.8 %copy.139 = bf16[2,2,2,4096]{3,1,0,2:T(2,128)(2,1)} copy(bf16[2,2,2,4096]{0,1,3,2:T(2,128)(2,1)} %bitcast.77) | data formatting | bytes 131072 | tf_op jit(solution)/shard_map/all_to_all | solution.py:71
  54.6 6.8 %copy.133 = bf16[2,1,8192]{0,1,2:T(2,128)(2,1)} copy(bf16[2,1,8192]{2,0,1:T(2,128)(2,1)S(1)} %bitcast.95) | data formatting | bytes 65536 | tf_op jit(solution)/shard_map/broadcast_in_dim | solution.py:78
  61.4 0.5 broadcast.47
  61.9 45.2 %reduce.6 = bf16[8192,2]{1,0:T(8,128)(2,1)S(1)} reduce(bf16[8192,1,2]{2,1,0:T(2,128)(2,1)} %bitcast.75, bf16[]{:T(256)} %broadcast.47), dimensions={1}, to_apply=%bitcast.53.reduce_sub_computation | reduce | bytes 65538
  107.1 3.8 %reshape.95 = bf16[2,2,4096]{2,1,0:T(2,128)(2,1)} reshape(bf16[8192,2]{1,0:T(8,128)(2,1)S(1)} %reduce.6) | data formatting | bytes 65536
  111.0 3.5 all-to-all-start.1
  114.5 0.1 dynamic_slice.10
  114.6 0.4 fusion.12
  115.0 0.1 pad_maximum_fusion
  115.1 0.1 fusion.19
  115.2 0.1 copy.161
  115.3 16.7 %copy.132 = bf16[1536,4096]{0,1:T(8,128)(2,1)} copy(bf16[1536,4096]{1,0:T(8,128)(2,1)} %param.15) | data formatting | bytes 25165824 | tf_op args[4]
  132.0 16.7 %copy.136 = bf16[1536,32,128]{2,0,1:T(8,128)(2,1)} copy(bf16[1536,32,128]{0,2,1:T(8,128)(2,1)} %bitcast.74) | data formatting | bytes 25165824 | tf_op jit(solution)/shard_map/concatenate | solution.py:93
  148.7 6.7 %copy.128 = bf16[2,2,8192]{0,1,2:T(2,128)(2,1)} copy(bf16[2,2,8192]{2,0,1:T(2,128)(2,1)S(1)} %pad_maximum_fusion) | data formatting | bytes 131072 | tf_op jit(solution)/shard_map/stack | solution.py:80
  155.4 9.6 %reshape.99 = bf16[2,2,8192]{2,1,0:T(2,128)(2,1)} reshape(bf16[8192,2,2]{2,1,0:T(2,128)(2,1)} %bitcast.78) | data formatting | bytes 131072
  165.0 3.3 all-to-all-start
  168.4 6.2 %reshape.96 = bf16[8192,1,2]{2,1,0:T(2,128)(2,1)} reshape(bf16[2,2,4096]{2,1,0:T(2,128)(2,1)S(1)} %all-to-all-done.1) | data formatting | bytes 65536
  174.6 8.1 %copy.134 = bf16[2,1,8192]{2,0,1:T(2,128)(2,1)S(1)} copy(bf16[2,1,8192]{0,1,2:T(2,128)(2,1)} %bitcast.79) | data formatting | bytes 65536 | tf_op jit(solution)/shard_map/all_to_all | solution.py:78
  182.8 1.9 reshape.90
  184.7 14.7 %fusion.4 = (f32[64,2,32]{0,1,2:T(2,128)S(1)}, f32[32,1540,64,2]{1,2,3,0:T(8,128)}) fusion(pred[64,1540]{1,0:T(8,128)(4,1)S(1)} %concatenate.20.clone, bf16[64,2,32,128]{3,2,1,0:T(8,128)(2,1)S(1)} %reshape.90, bf16[4,32,128]{2,0,1:T(4,128)(2,1)S(1)} %copy.137, bf16[1536,32,128]{2,0,1:T(8,128)(2,1)} %copy.136), kind=kOutput, calls=%fused_computation.7 | convolution fusion | flops 1658957824 | bytes 39010560 | tf_op jit(solution)/shard_map/while/body/eval_jaxpr/qshd,khd->qshk/dot_general | solution.py:23
  199.3 17.4 %convert_reduce_fusion = (f32[64,2,32]{0,1,2:T(2,128)S(1)}, bf16[64,2,32,1540]{3,0,1,2:T(8,128)(2,1)}) fusion(f32[64,2,32]{0,1,2:T(2,128)S(1)} %get-tuple-element.28, f32[32,1540,64,2]{1,2,3,0:T(8,128)} %get-tuple-element.29, pred[64,1540]{1,0:T(8,128)(4,1)S(1)} %concatenate.20.clone), kind=kLoop, calls=%fused_computation.1 | loop fusion | flops 37842944 | bytes 37978368 | tf_op jit(solution)/shard_map/while/body/eval_jaxpr/reduce_sum | solution.py:33
  216.8 0.1 copy.146
  216.9 0.7 reshape.101
  217.6 5.9 %all-to-all-start.4 = ((f32[16,1,256]{2,1,0:T(1,128)}), f32[16,1,256]{2,1,0:T(1,128)S(1)}, u32[]{:S(2)}, u32[]{:S(2)}) async-start(f32[16,1,256]{2,1,0:T(1,128)} %reshape.101), calls=%async_computation.4 | async-start | bytes 32768 | tf_op jit(solution)/shard_map/all_to_all | solution.py:122
  223.6 11.6 %copy_bitcast_fusion = bf16[1536,32,128]{2,0,1:T(8,128)(2,1)} fusion(bf16[1536,4096]{1,0:T(8,128)(2,1)} %param.16), kind=kLoop, calls=%fused_computation.13 | loop fusion | bytes 25165824 | tf_op jit(solution)/shard_map/broadcast_in_dim | solution.py:94
  235.2 10.4 %reshape.100 = bf16[8192,2,2]{2,1,0:T(2,128)(2,1)} reshape(bf16[2,2,8192]{2,1,0:T(2,128)(2,1)S(1)} %all-to-all-done) | data formatting | bytes 131072
  245.6 8.9 %copy.129 = bf16[2,2,2,4096]{3,1,0,2:T(2,128)(2,1)S(1)} copy(bf16[2,2,2,4096]{0,1,3,2:T(2,128)(2,1)} %bitcast.80) | data formatting | bytes 131072 | tf_op jit(solution)/shard_map/all_to_all | solution.py:79
  254.5 0.1 concatenate.18
  254.6 0.1 copy.130
  254.6 0.1 copy.148
  254.7 0.7 reshape.103
  255.5 6.0 %all-to-all-start.5 = ((f32[16,1,256]{2,1,0:T(1,128)}), f32[16,1,256]{2,1,0:T(1,128)S(1)}, u32[]{:S(2)}, u32[]{:S(2)}) async-start(f32[16,1,256]{2,1,0:T(1,128)} %reshape.103), calls=%async_computation.5 | async-start | bytes 32768 | tf_op jit(solution)/shard_map/all_to_all | solution.py:123
  261.5 16.4 %broadcast_in_dim.58 = bf16[1536,2,32,128]{3,0,2,1:T(8,128)(2,1)} broadcast(bf16[1536,32,128]{2,0,1:T(8,128)(2,1)} %copy_bitcast_fusion), dimensions={0,2,3} | broadcast | bytes 37748736 | tf_op jit(solution)/shard_map/broadcast_in_dim | solution.py:94
  277.9 14.1 %fusion.13 = bf16[64,2,32,128]{3,0,2,1:T(8,128)(2,1)S(1)} fusion(bf16[64,2,32,1540]{3,0,1,2:T(8,128)(2,1)} %get-tuple-element.27, bf16[4,2,32,128]{3,0,2,1:T(4,128)(2,1)S(1)} %copy.130, bf16[1536,2,32,128]{3,0,2,1:T(8,128)(2,1)} %broadcast_in_dim.58, f32[64,2,32]{0,2,1:T(8,128)S(1)} %copy.143), kind=kOutput, calls=%fused_computation.21 | convolution fusion | flops 1666318336 | bytes 38912000 | tf_op jit(solution)/shard_map/while/body/eval_jaxpr/qshk,kshd->qshd/dot_general | solution.py:34
  292.0 0.7 copy.157
  292.6 1.1 reshape.91
  293.8 6.0 %all-to-all-start.3 = ((bf16[1,64,2,4096]{3,2,0,1:T(2,128)(2,1)}), bf16[1,64,2,4096]{3,2,0,1:T(2,128)(2,1)S(1)}, u32[]{:S(2)}, u32[]{:S(2)}) async-start(bf16[1,64,2,4096]{3,2,0,1:T(2,128)(2,1)} %reshape.91), calls=%async_computation.3 | async-start | bytes 2097152 | tf_op jit(solution)/shard_map/all_to_all | solution.py:120
  299.8 0.5 broadcast.48
  300.3 0.7 reduce.7
  301.0 0.1 reshape.102
  301.1 0.7 reduce.8
  301.8 0.1 reshape.104
  302.0 0.1 copy.150
  302.1 20.6 %all-to-all-done.3 = bf16[1,64,2,4096]{3,2,0,1:T(2,128)(2,1)S(1)} async-done(((bf16[1,64,2,4096]{3,2,0,1:T(2,128)(2,1)}), bf16[1,64,2,4096]{3,2,0,1:T(2,128)(2,1)S(1)}, u32[]{:S(2)}, u32[]{:S(2)}) %all-to-all-start.3) | async-done | bytes 1048608 | tf_op jit(solution)/shard_map/all_to_all | solution.py:120
  322.7 0.7 reshape.88
  323.4 0.7 multiply_reduce_fusion
  324.2 0.1 divide_convert_fusion
  324.3 0.3 slice_reduce_fusion
  324.6 0.6 all_to_all.103
  325.2 3.3 all-to-all-start.6
  328.5 0.6 all_to_all.107
  329.1 3.3 all-to-all-done.6
  332.5 3.3 all-to-all-start.7
  335.7 3.9 %all-to-all-done.7 = bf16[2,2,4096]{2,1,0:T(2,128)(2,1)S(1)} async-done(((bf16[2,2,4096]{2,1,0:T(2,128)(2,1)}), bf16[2,2,4096]{2,1,0:T(2,128)(2,1)S(1)}, u32[]{:S(2)}, u32[]{:S(2)}) %all-to-all-start.7) | async-done | bytes 32800 | tf_op jit(solution)/shard_map/all_to_all | solution.py:137
  339.7 0.6 copy.176
  340.3 0.6 copy.177
  (34 shorter events, 0.4 us)
Async XLA Ops:
  7.2 1.0 copy-start
  7.2 47.4 %copy-start.2 = (bf16[2,8192]{1,0:T(2,128)(2,1)S(1)}, bf16[2,8192]{1,0:T(2,128)(2,1)}, u32[]{:S(2)}) copy-start(bf16[2,8192]{1,0:T(2,128)(2,1)} %param.13) | copy-start | bytes 98308
  7.2 175.6 %all-gather.2.cloned.1.call-start = ((), (), s32[]{:S(2)}) async-start(), calls=%async_computation.8 | async-start | bytes 1114112 | tf_op jit(solution)/shard_map/all_gather | solution.py:88
  17.2 97.3 %copy-start.4 = (s32[64]{0:T(128)S(1)}, s32[64]{0:T(128)}, u32[]{:S(2)}) copy-start(s32[64]{0:T(128)} %param.21) | copy-start | bytes 772
  17.2 97.3 %copy-start.3 = (bf16[2,8192]{1,0:T(2,128)(2,1)S(1)}, bf16[2,8192]{1,0:T(2,128)(2,1)}, u32[]{:S(2)}) copy-start(bf16[2,8192]{1,0:T(2,128)(2,1)} %param.14) | copy-start | bytes 98308
  17.2 97.3 %copy-start.5 = (bf16[16,8192]{1,0:T(8,128)(2,1)S(1)}, bf16[16,8192]{1,0:T(8,128)(2,1)}, u32[]{:S(2)}) copy-start(bf16[16,8192]{1,0:T(8,128)(2,1)} %param.20) | copy-start | bytes 786436
  17.2 97.3 %copy-start.6 = (bf16[8192,16]{0,1:T(8,128)(2,1)S(1)}, bf16[8192,16]{0,1:T(8,128)(2,1)}, u32[]{:S(2)}) copy-start(bf16[8192,16]{0,1:T(8,128)(2,1)} %param.19) | copy-start | bytes 786436
  17.2 97.3 %copy-start.7 = (bf16[2,8192]{1,0:T(2,128)(2,1)S(1)}, bf16[2,8192]{1,0:T(2,128)(2,1)}, u32[]{:S(2)}) copy-start(bf16[2,8192]{1,0:T(2,128)(2,1)} %param.11) | copy-start | bytes 98308
  111.0 54.1 %all-to-all-start.1 = ((bf16[2,2,4096]{2,1,0:T(2,128)(2,1)}), bf16[2,2,4096]{2,1,0:T(2,128)(2,1)S(1)}, u32[]{:S(2)}, u32[]{:S(2)}) async-start(bf16[2,2,4096]{2,1,0:T(2,128)(2,1)} %reshape.95), calls=%async_computation.1 | async-start | bytes 65536 | tf_op jit(solution)/shard_map/all_to_all | solution.py:78
  165.0 52.5 %all-to-all-start = ((bf16[2,2,8192]{2,1,0:T(2,128)(2,1)}), bf16[2,2,8192]{2,1,0:T(2,128)(2,1)S(1)}, u32[]{:S(2)}, u32[]{:S(2)}) async-start(bf16[2,2,8192]{2,1,0:T(2,128)(2,1)} %reshape.99), calls=%async_computation | async-start | bytes 131072 | tf_op jit(solution)/shard_map/all_to_all | solution.py:79
  217.6 37.9 %all-to-all-start.4 = ((f32[16,1,256]{2,1,0:T(1,128)}), f32[16,1,256]{2,1,0:T(1,128)S(1)}, u32[]{:S(2)}, u32[]{:S(2)}) async-start(f32[16,1,256]{2,1,0:T(1,128)} %reshape.101), calls=%async_computation.4 | async-start | bytes 32768 | tf_op jit(solution)/shard_map/all_to_all | solution.py:122
  255.5 38.3 %all-to-all-start.5 = ((f32[16,1,256]{2,1,0:T(1,128)}), f32[16,1,256]{2,1,0:T(1,128)S(1)}, u32[]{:S(2)}, u32[]{:S(2)}) async-start(f32[16,1,256]{2,1,0:T(1,128)} %reshape.103), calls=%async_computation.5 | async-start | bytes 32768 | tf_op jit(solution)/shard_map/all_to_all | solution.py:123
  277.9 63.0 %copy-start.1 = (bf16[16,8192]{1,0:T(8,128)(2,1)S(1)}, bf16[16,8192]{1,0:T(8,128)(2,1)}, u32[]{:S(2)}) copy-start(bf16[16,8192]{1,0:T(8,128)(2,1)} %param.18) | copy-start | bytes 786436
  293.8 29.0 %all-to-all-start.3 = ((bf16[1,64,2,4096]{3,2,0,1:T(2,128)(2,1)}), bf16[1,64,2,4096]{3,2,0,1:T(2,128)(2,1)S(1)}, u32[]{:S(2)}, u32[]{:S(2)}) async-start(bf16[1,64,2,4096]{3,2,0,1:T(2,128)(2,1)} %reshape.91), calls=%async_computation.3 | async-start | bytes 2097152 | tf_op jit(solution)/shard_map/all_to_all | solution.py:120
  325.2 7.2 %all-to-all-start.6 = ((bf16[2,2,4096]{2,1,0:T(2,128)(2,1)}), bf16[2,2,4096]{2,1,0:T(2,128)(2,1)S(1)}, u32[]{:S(2)}, u32[]{:S(2)}) async-start(bf16[2,2,4096]{2,1,0:T(2,128)(2,1)} %all_to_all.103), calls=%async_computation.6 | async-start | bytes 65536 | tf_op jit(solution)/shard_map/all_to_all | solution.py:136
  332.5 7.2 %all-to-all-start.7 = ((bf16[2,2,4096]{2,1,0:T(2,128)(2,1)}), bf16[2,2,4096]{2,1,0:T(2,128)(2,1)S(1)}, u32[]{:S(2)}, u32[]{:S(2)}) async-start(bf16[2,2,4096]{2,1,0:T(2,128)(2,1)} %all_to_all.107), calls=%async_computation.7 | async-start | bytes 65536 | tf_op jit(solution)/shard_map/all_to_all | solution.py:137
Sparse Core Ops, SparseCore 0:
  54.7 38.2 all-gather.1
where the time goes:
time: 351 us; the launch traced here: 348 us
  local copies, waits for them, and re-layouts  170 us (48%)
  other arithmetic  65.9 us (19%)
  starting transfers between devices  31.3 us (9%)
  matrix products  30.5 us (9%)
  waiting for transfers between devices  28 us (8%)
  between operations  14.4 us (4%)
  blocking collectives  8.13 us (2%)
    unnamed x31, local copies, waits for them, and re-layouts  70.6 us
    unnamed x1, other arithmetic  45.2 us
    broadcast_in_dim x2, local copies, waits for them, and re-layouts, local(): jnp.broadcast_to(prompt_values[:, None, :], (cache_rows, 2, group_width))  28 us
    all_to_all x1, waiting for transfers between devices, local(): lax.all_to_all(part_mean[None], 'ctx', split_axis=1, concat_axis=0, tiled...  20.6 us
    reduce_sum x1, other arithmetic, partial_block(): part_total = jnp.sum(probs.astype(jnp.float32), -1)  17.4 us
    concatenate x3, local copies, waits for them, and re-layouts, local(): jnp.concatenate([prompt_keys, stretch_keys], 0).reshape(-1, head_count, HD)  16.7 us
    dot_general x1, matrix products, partial_block(): jnp.einsum('qshd,khd->qshk', query_block, key_rows, preferred_element_typ...  14.7 us
    dot_general x1, matrix products, partial_block(): jnp.einsum('qshk,kshd->qshd', probs, value_rows, preferred_element_type=j...  14.1 us
  transfers between devices with their start and end apart: 8, of which 3 were waited for; matrix products, arithmetic and copies ran while one was open for 64% of the time, Pallas kernels for 0%

commit v1 on v0

v1 whole, which is shorter than its diff:
```python
import functools

import jax
import jax.numpy as jnp
from jax import lax
from jax.experimental import pallas as pl
from jax.experimental.pallas import tpu as pltpu
from jax.sharding import PartitionSpec as P

HD = 128
LOG2E = 1.4426950408889634
F32 = jnp.float32
BF16 = jnp.bfloat16
MESH = pl.DeviceIdType.MESH


def dot(a, b):
    return jnp.dot(a, b, preferred_element_type=F32)


def dot_t(a, b):
    return lax.dot_general(a, b, (((1,), (1,)), ((), ())), preferred_element_type=F32)


def iota(shape, dim):
    return lax.broadcasted_iota(jnp.int32, shape, dim)


def kernel(
    n, g, tdev, steps,
    idx_ref, in_ref, q_ref, k_ref, v_ref, pk_hbm, pv_hbm, qd_ref, qu_ref, vd_ref, vu_ref,
    outa_ref, outb_ref,
    msgf, msg, kmsg, vmsg, gbuf, kx, vx, kbuf, vbuf, maskbuf, qbuf, kext, vext,
    obuf, rc, cbuf, ry, zbuf, rz, xbuf, rx,
    sem_kv, sx, rxs, sz, rzs, sy, rys, sc, rcs,
    scs, rcr, sys_, ryr, szs, rzr, sxs, rxr,
):
    c = lax.axis_index("ctx")
    h = lax.axis_index("head")
    nz = n // 4
    z = lax.div(c, 4)
    y = lax.rem(lax.div(c, 2), 2)
    core = lax.rem(c, 2)
    gw = pk_hbm.shape[1]
    chunks = 16 // tdev
    cjw = gw // chunks
    jper = chunks // steps
    cw = cjw * jper
    hc = cw // HD
    ng = n * g
    rows_slot = 2 * tdev
    rows = ng * rows_slot
    r1, r2 = rows // 2, rows // 4
    rc_rows = g * rows_slot
    fold = 1 if rc_rows >= 16 else 16 // rc_rows
    cache = pk_hbm.shape[0]
    blk = obuf.shape[1] if obuf.shape[1] < 128 else 128
    sb = blk // rows_slot
    nblk = rows // blk
    ext = g * rows_slot
    extp = kext.shape[1]
    tokens = ng * tdev

    def ctx_of(zz, yy, cc):
        return zz * 4 + yy * 2 + cc

    def slot_of(zz, yy, cc):
        return ((cc * 2 + yy) * nz + zz) * g

    def kv_copies(s):
        cols = pl.ds(s * cw, cw)
        return (
            pltpu.make_async_copy(pk_hbm.at[:, cols], kbuf.at[s], sem_kv.at[0, s]),
            pltpu.make_async_copy(pv_hbm.at[:, cols], vbuf.at[s], sem_kv.at[1, s]),
        )

    for s in range(steps):
        for cp in kv_copies(s):
            cp.start()

    barrier = pltpu.get_barrier_semaphore()
    sib = (ctx_of(z, y, 1 - core), h)
    ynb = (ctx_of(z, 1 - y, core), h)
    znb = [(ctx_of(lax.rem(z + d, nz), y, core), h) for d in range(1, nz)]
    xnb = [(c, lax.rem(h + d, g)) for d in range(1, g)]
    partners = [sib, ynb] + znb + xnb
    for p in partners:
        pl.semaphore_signal(barrier, inc=1, device_id=p, device_id_type=MESH)

    up_q = dot_t(in_ref[...], qd_ref[...])
    up_v = dot_t(in_ref[...], vd_ref[...])
    rank = up_q.shape[1]
    qf, kf, vf = (r[...].astype(F32) for r in (q_ref, k_ref, v_ref))
    msgf[...] = jnp.zeros(msgf.shape, F32)
    msgf[0:tdev, cjw:cjw + rank] = up_q
    msgf[tdev:2 * tdev, cjw:cjw + rank] = up_v
    for p in range(g):
        for src, dst in ((kf, kmsg), (vf, vmsg), (qf, msg)):
            for j in range(chunks):
                at = p * gw + j * cjw
                msgf[j * tdev:(j + 1) * tdev, 0:cjw] = src[:, at:at + cjw]
            if dst is msg:
                dst[p] = msgf[...].astype(BF16)
            else:
                dst[p] = msgf[:, 0:cjw].astype(BF16)

    pl.semaphore_wait(barrier, len(partners))

    my_slot = slot_of(z, y, core)

    def remote(src, dst, ss, rs, dev):
        return pltpu.make_async_remote_copy(
            src_ref=src, dst_ref=dst, send_sem=ss, recv_sem=rs, device_id=dev, device_id_type=MESH
        )

    gx = []
    for d in range(1, g):
        p = lax.rem(h + d, g)
        gx.append(remote(msg.at[p], gbuf.at[my_slot + h], sx.at[d, 0], rxs.at[d, 0], xnb[d - 1]))
        gx.append(remote(kmsg.at[p], kx.at[h], sx.at[d, 1], rxs.at[d, 1], xnb[d - 1]))
        gx.append(remote(vmsg.at[p], vx.at[h], sx.at[d, 2], rxs.at[d, 2], xnb[d - 1]))
    for cp in gx:
        cp.start()
    gbuf[my_slot + h] = msg[h]
    kx[h] = kmsg[h]
    vx[h] = vmsg[h]
    for cp in gx:
        cp.wait_recv()

    here = gbuf.at[pl.ds(my_slot, g)]
    gz = [remote(here, here, sz.at[d], rzs.at[d], znb[d - 1]) for d in range(1, nz)]
    for cp in gz:
        cp.start()

    def pick(rows_out, j, width, per):
        rr = iota((rows_out, width), 0)
        cc = iota((rows_out, width), 1)
        sl = lax.div(rr, per)
        return rr, cc, sl

    def ext_select(j):
        rr = iota((extp, g * 16), 0)
        cc = iota((extp, g * 16), 1)
        rem = lax.rem(rr, g * tdev)
        want = lax.div(rem, tdev) * 16 + j * tdev + lax.rem(rem, tdev)
        return jnp.where((cc == want) & (rr < ext), 1.0, 0.0).astype(BF16)

    own = gbuf[pl.ds(my_slot, g)].reshape(g * 16, cjw + HD)
    av = dot(ext_select(1), own[:, cjw:])
    av = jnp.where(iota((extp, HD), 0) < g * tdev, av, 0.0).astype(BF16)[:, 0:rank]
    kxa = kx[...].reshape(g * 16, cjw)
    vxa = vx[...].reshape(g * 16, cjw)
    group_at = pl.multiple_of(h * gw, gw)
    for j in range(chunks):
        sel = ext_select(j)
        s, lo = j // jper, (j % jper) * cjw
        kext[s, :, lo:lo + cjw] = dot(sel, kxa).astype(BF16)
        wv = vu_ref[:, pl.ds(pl.multiple_of(group_at + j * cjw, 128), cjw)]
        vext[s, :, lo:lo + cjw] = (dot(sel, vxa) + dot(av, wv)).astype(BF16)

    idx_row = idx_ref[...].astype(F32)
    eye = iota((tokens, tokens), 0) == iota((tokens, tokens), 1)
    idx_col = jnp.sum(jnp.where(eye, idx_row, 0.0), axis=1, keepdims=True)
    tok_u0 = c * (g * tdev) + lax.rem(iota((tokens, extp), 1), g * tdev)
    seg_u = jnp.sum(
        jnp.where(iota((tokens, extp), 0) == tok_u0, idx_col, 0.0), axis=0, keepdims=True
    )

    def row_tokens(shape, b):
        r = iota(shape, 0) + b * blk
        sl = lax.div(r, rows_slot)
        hh = lax.rem(sl, g)
        place = lax.div(sl, g)
        zz = lax.rem(place, nz)
        yc = lax.div(place, nz)
        ctx = zz * 4 + lax.rem(yc, 2) * 2 + lax.div(yc, 2)
        return (ctx * g + hh) * tdev + lax.rem(r, tdev), lax.rem(lax.div(r, tdev), 2)

    def mask_block(b, carry):
        tok_r, unused = row_tokens((blk, tokens), b)
        seg_r = jnp.sum(
            jnp.where(iota((blk, tokens), 1) == tok_r, idx_row, 0.0), axis=1, keepdims=True
        )
        tok, stream = row_tokens((blk, extp), b)
        u = iota((blk, extp), 1)
        tok_u = c * (g * tdev) + lax.rem(u, g * tdev)
        ok = (u < ext) & (lax.div(u, g * tdev) == stream) & (tok_u <= tok) & (seg_r == seg_u)
        maskbuf[pl.ds(pl.multiple_of(b * blk, blk), blk), :] = jnp.where(ok, 1.0, 0.0)
        return carry

    lax.fori_loop(0, nblk, mask_block, 0)

    for cp in gz:
        cp.wait_recv()
    half = gbuf.at[pl.ds((core * 2 + y) * (nz * g), nz * g)]
    gy = remote(half, half, sy.at[0], rys.at[0], ynb)
    gy.start()
    gy.wait_recv()
    side = gbuf.at[pl.ds(core * (2 * nz * g), 2 * nz * g)]
    gc = remote(side, side, sc.at[0], rcs.at[0], sib)
    gc.start()
    gc.wait_recv()

    def q_select(j):
        rr = iota((blk, sb * 16), 0)
        cc = iota((blk, sb * 16), 1)
        want = lax.div(rr, rows_slot) * 16 + j * tdev + lax.rem(rr, tdev)
        return jnp.where(cc == want, 1.0, 0.0).astype(BF16)

    def q_block(b, carry):
        x = gbuf[pl.ds(b * sb, sb)].reshape(sb * 16, cjw + HD)
        a = dot(q_select(0), x[:, cjw:])
        first = lax.rem(lax.div(iota((blk, HD), 0), tdev), 2) == 0
        a = jnp.where(first, a, 0.0).astype(BF16)[:, 0:rank]
        at = pl.ds(pl.multiple_of(b * blk, blk), blk)
        for j in range(chunks):
            wq = qu_ref[:, pl.ds(pl.multiple_of(group_at + j * cjw, 128), cjw)]
            s, lo = j // jper, (j % jper) * cjw
            qbuf[s, at, lo:lo + cjw] = (dot(q_select(j), x[:, 0:cjw]) + dot(a, wq)).astype(BF16)
        return carry

    lax.fori_loop(0, nblk, q_block, 0)

    scale2 = HD ** (-0.5) * LOG2E

    def pack_lse(cols_of, r):
        lane = iota((r, HD), 1)
        which = lax.rem(lane, hc)
        x = jnp.zeros((r, HD), F32)
        for i in range(hc):
            x = jnp.where(which == i, cols_of(i), x)
        hi = x.astype(BF16).astype(F32)
        mid = (x - hi).astype(BF16).astype(F32)
        lo = x - hi - mid
        x = jnp.where(lane < hc, hi, jnp.where(lane < 2 * hc, mid, lo))
        return jnp.where(lane < 3 * hc, x, 0.0)

    def spread(x):
        lane, col = iota((HD, cw), 0), iota((HD, cw), 1)
        e = (lax.rem(lane, hc) == lax.div(col, HD)) & (lane < 3 * hc)
        return dot(x.astype(BF16), jnp.where(e, 1.0, 0.0).astype(BF16))

    def merge(parts):
        ls = [spread(p[:, cw:]) for p in parts]
        top = functools.reduce(jnp.maximum, ls)
        ws = [jnp.exp2(x - top) for x in ls]
        den = functools.reduce(jnp.add, ws)
        num = functools.reduce(jnp.add, [w * p[:, 0:cw].astype(F32) for w, p in zip(ws, parts)])
        return num / den, top + jnp.log2(den)

    def compute(s):
        for cp in kv_copies(s):
            cp.wait()

        def block(b, carry):
            at = pl.ds(pl.multiple_of(b * blk, blk), blk)
            seen = maskbuf[at, :] > 0.5
            lses = []
            for i in range(hc):
                cols = slice(i * HD, (i + 1) * HD)
                q = qbuf[s, at, cols]
                sp = dot_t(q, kbuf[s, :, cols])
                se = jnp.where(seen, dot_t(q, kext[s, :, cols]), -jnp.inf)
                m = jnp.maximum(
                    jnp.max(sp, axis=1, keepdims=True), jnp.max(se, axis=1, keepdims=True)
                ) * scale2
                pp = jnp.exp2(sp * scale2 - m)
                pe = jnp.exp2(se * scale2 - m)
                total = jnp.sum(pp, axis=1, keepdims=True) + jnp.sum(pe, axis=1, keepdims=True)
                o = dot(pp.astype(BF16), vbuf[s, :, cols]) + dot(pe.astype(BF16), vext[s, :, cols])
                obuf[s, at, cols] = (o / total).astype(BF16)
                lses.append(m + jnp.log2(total))
            obuf[s, at, cw:] = pack_lse(lambda i: lses[i], blk).astype(BF16)
            return carry

        lax.fori_loop(0, nblk, block, 0)

    def send_c(s):
        src = obuf.at[s, pl.ds(pl.multiple_of((1 - core) * r1, r1), r1)]
        return remote(src, rc.at[s], scs.at[s], rcr.at[s], sib)

    def send_y(s):
        src = cbuf.at[s, pl.ds(pl.multiple_of((1 - y) * r2, r2), r2)]
        return remote(src, ry.at[s], sys_.at[s], ryr.at[s], ynb)

    def send_z(s, d):
        return remote(
            zbuf.at[s, lax.rem(z + d, nz)], rz.at[s, d - 1], szs.at[s, d - 1], rzr.at[s, d - 1],
            znb[d - 1],
        )

    def send_x(s, d):
        return remote(
            xbuf.at[s], rx.at[s, d - 1], sxs.at[s, d - 1], rxr.at[s, d - 1], xnb[d - 1]
        )

    def merge_c(s):
        send_c(s).wait_recv()
        mine = obuf[s, pl.ds(pl.multiple_of(core * r1, r1), r1), :]
        o, l = merge([mine, rc[s]])
        cbuf[s, :, 0:cw] = o.astype(BF16)
        cbuf[s, :, cw:] = pack_lse(lambda i: l[:, i * HD:(i + 1) * HD], r1).astype(BF16)
        send_y(s).start()

    piece = cw // fold

    def fold_rows(x):
        return jnp.concatenate([x[:, f * piece:(f + 1) * piece] for f in range(fold)], axis=0)

    def unfold_rows(x):
        return jnp.concatenate(
            [x[f * rc_rows:(f + 1) * rc_rows, 0:piece] for f in range(fold)], axis=1
        )

    def merge_y(s):
        send_y(s).wait_recv()
        mine = cbuf[s, pl.ds(pl.multiple_of(y * r2, r2), r2), :]
        o, l = merge([mine, ry[s]])
        packed = pack_lse(lambda i: l[:, i * HD:(i + 1) * HD], r2)
        for zz in range(nz):
            at = slice(zz * rc_rows, (zz + 1) * rc_rows)
            zbuf[s, zz, :, 0:piece] = fold_rows(o[at, :]).astype(BF16)
            zbuf[s, zz, :, piece:] = jnp.concatenate([packed[at, :]] * fold, axis=0).astype(BF16)
        for d in range(1, nz):
            send_z(s, d).start()

    def merge_z(s):
        parts = []
        for d in range(nz):
            if d:
                send_z(s, d).wait_recv()
                x = rz[s, d - 1].astype(F32)
            else:
                x = zbuf[s, z].astype(F32)
            parts.append(jnp.concatenate([unfold_rows(x), x[0:rc_rows, piece:]], axis=1))
        o, unused = merge(parts)
        xbuf[s] = fold_rows(o).astype(BF16)
        for d in range(1, g):
            send_x(s, d).start()

    def write(x, group, s):
        x = unfold_rows(x.astype(F32))
        mine = x[0:rows_slot]
        for p in range(1, g):
            mine = jnp.where(h == p, x[p * rows_slot:(p + 1) * rows_slot], mine)
        cols = pl.ds(pl.multiple_of(group * gw + s * cw, 128), cw)
        outa_ref[:, cols] = mine[0:tdev].astype(BF16)
        outb_ref[:, cols] = mine[tdev:rows_slot].astype(BF16)

    def turn(t, carry):
        @pl.when(t < steps)
        def _():
            compute(t)
            send_c(t).start()

        @pl.when((t >= 1) & (t < steps + 1))
        def _():
            merge_c(t - 1)

        @pl.when((t >= 2) & (t < steps + 2))
        def _():
            merge_y(t - 2)

        @pl.when(t >= 3)
        def _():
            merge_z(t - 3)

        return carry

    lax.fori_loop(0, steps + 3, turn, 0)

    def finish(s, carry):
        write(xbuf[s], h, s)
        for d in range(1, g):
            send_x(s, d).wait_recv()
            write(rx[s, d - 1], lax.rem(h + g - d, g), s)
            send_x(s, d).wait_send()
        send_c(s).wait_send()
        send_y(s).wait_send()
        for d in range(1, nz):
            send_z(s, d).wait_send()
        return carry

    lax.fori_loop(0, steps, finish, 0)
    for cp in gx + gz + [gy, gc]:
        cp.wait_send()


def local(
    response_input, response_queries, response_keys, response_values, prompt_keys, prompt_values,
    query_down_weight, query_up_weight, value_down_weight, value_up_weight, response_index,
):
    n = lax.axis_size("ctx")
    g = lax.axis_size("head")
    tdev, width = response_input.shape
    cache, gw = prompt_keys.shape
    chunks = 16 // tdev
    cjw = gw // chunks
    steps = chunks if cjw >= 256 else chunks // 2
    cw = gw // steps
    mw = cw + HD
    nz = n // 4
    ng = n * g
    rows = ng * 2 * tdev
    rc_rows = 2 * tdev * g
    fold = 1 if rc_rows >= 16 else 16 // rc_rows
    zr = rc_rows * fold
    extp = -(-2 * tdev * g // 16) * 16
    vmem = pl.BlockSpec(memory_space=pltpu.VMEM)
    hbm = pl.BlockSpec(memory_space=pl.ANY)
    dma = pltpu.SemaphoreType.DMA
    out = jax.ShapeDtypeStruct((tdev, width), BF16)
    return pl.pallas_call(
        functools.partial(kernel, n, g, tdev, steps),
        out_shape=(out, out),
        in_specs=[vmem, vmem, vmem, vmem, vmem, hbm, hbm, vmem, vmem, vmem, vmem],
        out_specs=(vmem, vmem),
        scratch_shapes=[
            pltpu.VMEM((16, cjw + HD), F32),
            pltpu.VMEM((g, 16, cjw + HD), BF16),
            pltpu.VMEM((g, 16, cjw), BF16),
            pltpu.VMEM((g, 16, cjw), BF16),
            pltpu.VMEM((ng, 16, cjw + HD), BF16),
            pltpu.VMEM((g, 16, cjw), BF16),
            pltpu.VMEM((g, 16, cjw), BF16),
            pltpu.VMEM((steps, cache, cw), BF16),
            pltpu.VMEM((steps, cache, cw), BF16),
            pltpu.VMEM((rows, extp), F32),
            pltpu.VMEM((steps, rows, cw), BF16),
            pltpu.VMEM((steps, extp, cw), BF16),
            pltpu.VMEM((steps, extp, cw), BF16),
            pltpu.VMEM((steps, rows, mw), BF16),
            pltpu.VMEM((steps, rows // 2, mw), BF16),
            pltpu.VMEM((steps, rows // 2, mw), BF16),
            pltpu.VMEM((steps, rows // 4, mw), BF16),
            pltpu.VMEM((steps, nz, zr, cw // fold + HD), BF16),
            pltpu.VMEM((steps, nz - 1, zr, cw // fold + HD), BF16),
            pltpu.VMEM((steps, zr, cw // fold), BF16),
            pltpu.VMEM((steps, g - 1, zr, cw // fold), BF16),
            dma((2, steps)),
            dma((g, 3)), dma((g, 3)), dma((nz,)), dma((nz,)),
            dma((1,)), dma((1,)), dma((1,)), dma((1,)),
            dma((steps,)), dma((steps,)), dma((steps,)), dma((steps,)),
            dma((steps, nz - 1)), dma((steps, nz - 1)),
            dma((steps, g - 1)), dma((steps, g - 1)),
        ],
        compiler_params=pltpu.CompilerParams(
            collective_id=0, has_side_effects=True, vmem_limit_bytes=60 * 1024 * 1024
        ),
    )(
        response_index.reshape(1, -1), response_input, response_queries, response_keys,
        response_values, prompt_keys, prompt_values, query_down_weight.T, query_up_weight,
        value_down_weight.T, value_up_weight,
    )


def solution(mesh):
    token = P(("ctx", "head"), None)
    return jax.shard_map(
        local,
        mesh=mesh,
        in_specs=(token, token, token, token, P("ctx", "head"), P("ctx", "head"))
        + (P(),) * 5,
        out_specs=(token, token),
        check_vma=False,
    )
```

time: 351 us -> 59.6 us (0.17)
  local copies, waits for them, and re-layouts: 170 us -> 2.79 us
  other arithmetic: 65.9 us -> 0 us
  Pallas kernels: 0 us -> 55.9 us
  starting transfers between devices: 31.3 us -> 0 us
  matrix products: 30.5 us -> 0 us
  waiting for transfers between devices: 28 us -> 0 us
  between operations: 14.4 us -> 0.64 us
  blocking collectives: 8.13 us -> 0 us
    unnamed x31 -> x2, local copies, waits for them, and re-layouts: 70.6 us -> 2.79 us
    pallas_call x0 -> x1, Pallas kernels: none -> 55.9 us  [local(): pl.pallas_call(functools.partial(kernel, n, g, tdev, steps), out_shape=(o...]
    unnamed x1 -> x0, other arithmetic: 45.2 us -> none
    broadcast_in_dim x5 -> x0, local copies, waits for them, and re-layouts: 35 us -> none  [the longest x2 28 us: local(): jnp.broadcast_to(prompt_values[:, None, :], (cache_rows, 2, group_width))]
    all_to_all x7 -> x0, starting transfers between devices: 31.3 us -> none  [the longest x1 6.01 us: local(): lax.all_to_all(part_mean[None], 'ctx', split_axis=1, concat_axis=0, tiled...]
    dot_general x4 -> x0, matrix products: 30.5 us -> none  [the longest x1 14.7 us: partial_block(): jnp.einsum('qshd,khd->qshk', query_block, key_rows, preferred_element_typ...]
    all_to_all x10 -> x0, local copies, waits for them, and re-layouts: 28.6 us -> none  [the longest x1 9.79 us: local(): lax.all_to_all(jnp.stack([query_with_adapter, response_queries], 1), 'hea...]
    all_to_all x7 -> x0, waiting for transfers between devices: 27.9 us -> none  [the longest x1 20.6 us: local(): lax.all_to_all(part_mean[None], 'ctx', split_axis=1, concat_axis=0, tiled...]
  transfers between devices with their start and end apart: 8 -> 0, of which waited for: 3 -> 0; matrix products, arithmetic and copies ran while one was open for 64% -> 0% of each run, Pallas kernels for 0% -> 0%
where the time goes in v1:
time: 59.6 us; the launch traced here: 59.3 us
  Pallas kernels  55.9 us (94%)
  local copies, waits for them, and re-layouts  2.79 us (5%)
  between operations  0.64 us (1%)
    pallas_call x1, Pallas kernels, local(): pl.pallas_call(functools.partial(kernel, n, g, tdev, steps), out_shape=(o...  55.9 us
    unnamed x2, local copies, waits for them, and re-layouts  2.79 us

profile of v1, /device:TPU:0, one launch (start us, length us, event | category | flops | bytes accessed | tf_op | source)
XLA Modules:
  0.0 59.3 jit_solution(10812033897237615797)
XLA Ops:
  0.6 55.9 %shard_map.122 = (bf16[2,8192]{1,0:T(2,128)(2,1)}, bf16[2,8192]{1,0:T(2,128)(2,1)}) custom-call(s32[1,64]{1,0:T(1,128)} %bitcast.5, bf16[2,8192]{1,0:T(2,128)(2,1)} %in_ref.1, bf16[2,8192]{1,0:T(2,128)(2,1)} %q_ref.1, bf16[2,8192]{1,0:T(2,128)(2,1)} %k_ref.1, bf16[2,8192]{1,0:T(2,128)(2,1)} %v_ref.1, bf16[1536,4096]{1,0:T(8,128)(2,1)} %pk_hbm.1, ...), custom_call_target="tpu_custom_call" | custom-call | tf_op jit(solution)/shard_map/pallas_call | solution.py:413
  56.5 1.4 %copy.15 = bf16[2,8192]{1,0:T(2,128)(2,1)} copy(bf16[2,8192]{1,0:T(2,128)(2,1)} %get-tuple-element.4) | data formatting | bytes 65536
  57.9 1.4 %copy.16 = bf16[2,8192]{1,0:T(2,128)(2,1)} copy(bf16[2,8192]{1,0:T(2,128)(2,1)} %get-tuple-element.5) | data formatting | bytes 65536

commit v2 on v1

--- a/solution.py
+++ b/solution.py
@@ -26,12 +26,22 @@
     return lax.broadcasted_iota(jnp.int32, shape, dim)
 
 
+def vdiv(x, d):
+    if d & (d - 1):
+        return lax.div(x, d)
+    return lax.shift_right_logical(x, jnp.int32(d.bit_length() - 1)) if d > 1 else x
+
+
+def vrem(x, d):
+    return lax.rem(x, d) if d & (d - 1) else x & (d - 1)
+
+
 def kernel(
     n, g, tdev, steps,
     idx_ref, in_ref, q_ref, k_ref, v_ref, pk_hbm, pv_hbm, qd_ref, qu_ref, vd_ref, vu_ref,
     outa_ref, outb_ref,
     msgf, msg, kmsg, vmsg, gbuf, kx, vx, kbuf, vbuf, maskbuf, qbuf, kext, vext,
-    obuf, rc, cbuf, ry, zbuf, rz, xbuf, rx,
+    obuf, rc, cbuf, ry, zbuf, rz, xbuf, rx, spread_ref,
     sem_kv, sx, rxs, sz, rzs, sy, rys, sc, rcs,
     scs, rcr, sys_, ryr, szs, rzr, sxs, rxr,
 ):
@@ -131,19 +141,26 @@
     gz = [remote(here, here, sz.at[d], rzs.at[d], znb[d - 1]) for d in range(1, nz)]
     for cp in gz:
         cp.start()
-
-    def pick(rows_out, j, width, per):
-        rr = iota((rows_out, width), 0)
-        cc = iota((rows_out, width), 1)
-        sl = lax.div(rr, per)
-        return rr, cc, sl
+    gy, gc = [], []
+    for d in range(nz):
+        zs = lax.rem(z + nz - d, nz)
+        part = gbuf.at[pl.ds(slot_of(zs, y, core), g)]
+        gy.append(remote(part, part, sy.at[d], rys.at[d], ynb))
+        gc.append(remote(part, part, sc.at[d], rcs.at[d], sib))
+    for d in range(nz):
+        zs = lax.rem(z + nz - d, nz)
+        part = gbuf.at[pl.ds(slot_of(zs, 1 - y, core), g)]
+        gc.append(remote(part, part, sc.at[nz + d], rcs.at[nz + d], sib))
+    gy[0].start()
+    gc[0].start()
+
+    rr = iota((extp, g * 16), 0)
+    rem = vrem(rr, g * tdev)
+    ext_off = iota((extp, g * 16), 1) - (vdiv(rem, tdev) * 16 + vrem(rem, tdev))
+    ext_off = jnp.where(rr < ext, ext_off, -1)
 
     def ext_select(j):
-        rr = iota((extp, g * 16), 0)
-        cc = iota((extp, g * 16), 1)
-        rem = lax.rem(rr, g * tdev)
-        want = lax.div(rem, tdev) * 16 + j * tdev + lax.rem(rem, tdev)
-        return jnp.where((cc == want) & (rr < ext), 1.0, 0.0).astype(BF16)
+        return jnp.where(ext_off == j * tdev, 1.0, 0.0).astype(BF16)
 
     own = gbuf[pl.ds(my_slot, g)].reshape(g * 16, cjw + HD)
     av = dot(ext_select(1), own[:, cjw:])
@@ -158,23 +175,29 @@
         wv = vu_ref[:, pl.ds(pl.multiple_of(group_at + j * cjw, 128), cjw)]
         vext[s, :, lo:lo + cjw] = (dot(sel, vxa) + dot(av, wv)).astype(BF16)
 
+    rr = iota((blk, sb * 16), 0)
+    q_off = iota((blk, sb * 16), 1) - (vdiv(rr, rows_slot) * 16 + vrem(rr, tdev))
+    lane, col = iota((HD, cw), 0), iota((HD, cw), 1)
+    e = (vrem(lane, hc) == vdiv(col, HD)) & (lane < 3 * hc)
+    spread_ref[...] = jnp.where(e, 1.0, 0.0).astype(BF16)
+
     idx_row = idx_ref[...].astype(F32)
     eye = iota((tokens, tokens), 0) == iota((tokens, tokens), 1)
     idx_col = jnp.sum(jnp.where(eye, idx_row, 0.0), axis=1, keepdims=True)
-    tok_u0 = c * (g * tdev) + lax.rem(iota((tokens, extp), 1), g * tdev)
+    tok_u0 = c * (g * tdev) + vrem(iota((tokens, extp), 1), g * tdev)
     seg_u = jnp.sum(
         jnp.where(iota((tokens, extp), 0) == tok_u0, idx_col, 0.0), axis=0, keepdims=True
     )
 
     def row_tokens(shape, b):
         r = iota(shape, 0) + b * blk
-        sl = lax.div(r, rows_slot)
-        hh = lax.rem(sl, g)
-        place = lax.div(sl, g)
-        zz = lax.rem(place, nz)
-        yc = lax.div(place, nz)
-        ctx = zz * 4 + lax.rem(yc, 2) * 2 + lax.div(yc, 2)
-        return (ctx * g + hh) * tdev + lax.rem(r, tdev), lax.rem(lax.div(r, tdev), 2)
+        sl = vdiv(r, rows_slot)
+        hh = vrem(sl, g)
+        place = vdiv(sl, g)
+        zz = vrem(place, nz)
+        yc = vdiv(place, nz)
+        ctx = zz * 4 + vrem(yc, 2) * 2 + vdiv(yc, 2)
+        return (ctx * g + hh) * tdev + vrem(r, tdev), vrem(vdiv(r, tdev), 2)
 
     def mask_block(b, carry):
         tok_r, unused = row_tokens((blk, tokens), b)
@@ -183,34 +206,30 @@
         )
         tok, stream = row_tokens((blk, extp), b)
         u = iota((blk, extp), 1)
-        tok_u = c * (g * tdev) + lax.rem(u, g * tdev)
-        ok = (u < ext) & (lax.div(u, g * tdev) == stream) & (tok_u <= tok) & (seg_r == seg_u)
+        tok_u = c * (g * tdev) + vrem(u, g * tdev)
+        ok = (u < ext) & (vdiv(u, g * tdev) == stream) & (tok_u <= tok) & (seg_r == seg_u)
         maskbuf[pl.ds(pl.multiple_of(b * blk, blk), blk), :] = jnp.where(ok, 1.0, 0.0)
         return carry
 
     lax.fori_loop(0, nblk, mask_block, 0)
 
-    for cp in gz:
+    for d in range(1, nz):
+        gz[d - 1].wait_recv()
+        gy[d].start()
+        gc[d].start()
+    for d in range(nz):
+        gy[d].wait_recv()
+        gc[nz + d].start()
+    for cp in gc:
         cp.wait_recv()
-    half = gbuf.at[pl.ds((core * 2 + y) * (nz * g), nz * g)]
-    gy = remote(half, half, sy.at[0], rys.at[0], ynb)
-    gy.start()
-    gy.wait_recv()
-    side = gbuf.at[pl.ds(core * (2 * nz * g), 2 * nz * g)]
-    gc = remote(side, side, sc.at[0], rcs.at[0], sib)
-    gc.start()
-    gc.wait_recv()
 
     def q_select(j):
-        rr = iota((blk, sb * 16), 0)
-        cc = iota((blk, sb * 16), 1)
-        want = lax.div(rr, rows_slot) * 16 + j * tdev + lax.rem(rr, tdev)
-        return jnp.where(cc == want, 1.0, 0.0).astype(BF16)
+        return jnp.where(q_off == j * tdev, 1.0, 0.0).astype(BF16)
 
     def q_block(b, carry):
         x = gbuf[pl.ds(b * sb, sb)].reshape(sb * 16, cjw + HD)
         a = dot(q_select(0), x[:, cjw:])
-        first = lax.rem(lax.div(iota((blk, HD), 0), tdev), 2) == 0
+        first = vrem(vdiv(iota((blk, HD), 0), tdev), 2) == 0
         a = jnp.where(first, a, 0.0).astype(BF16)[:, 0:rank]
         at = pl.ds(pl.multiple_of(b * blk, blk), blk)
         for j in range(chunks):
@@ -225,7 +244,7 @@
 
     def pack_lse(cols_of, r):
         lane = iota((r, HD), 1)
-        which = lax.rem(lane, hc)
+        which = vrem(lane, hc)
         x = jnp.zeros((r, HD), F32)
         for i in range(hc):
             x = jnp.where(which == i, cols_of(i), x)
@@ -236,9 +255,7 @@
         return jnp.where(lane < 3 * hc, x, 0.0)
 
     def spread(x):
-        lane, col = iota((HD, cw), 0), iota((HD, cw), 1)
-        e = (lax.rem(lane, hc) == lax.div(col, HD)) & (lane < 3 * hc)
-        return dot(x.astype(BF16), jnp.where(e, 1.0, 0.0).astype(BF16))
+        return dot(x.astype(BF16), spread_ref[...])
 
     def merge(parts):
         ls = [spread(p[:, cw:]) for p in parts]
@@ -382,7 +399,7 @@
         return carry
 
     lax.fori_loop(0, steps, finish, 0)
-    for cp in gx + gz + [gy, gc]:
+    for cp in gx + gz + gy + gc:
         cp.wait_send()
 
 
@@ -396,7 +413,7 @@
     cache, gw = prompt_keys.shape
     chunks = 16 // tdev
     cjw = gw // chunks
-    steps = chunks if cjw >= 256 else chunks // 2
+    steps = chunks // 2
     cw = gw // steps
     mw = cw + HD
     nz = n // 4
@@ -437,9 +454,10 @@
             pltpu.VMEM((steps, nz - 1, zr, cw // fold + HD), BF16),
             pltpu.VMEM((steps, zr, cw // fold), BF16),
             pltpu.VMEM((steps, g - 1, zr, cw // fold), BF16),
+            pltpu.VMEM((HD, cw), BF16),
             dma((2, steps)),
             dma((g, 3)), dma((g, 3)), dma((nz,)), dma((nz,)),
-            dma((1,)), dma((1,)), dma((1,)), dma((1,)),
+            dma((nz,)), dma((nz,)), dma((2 * nz,)), dma((2 * nz,)),
             dma((steps,)), dma((steps,)), dma((steps,)), dma((steps,)),
             dma((steps, nz - 1)), dma((steps, nz - 1)),
             dma((steps, g - 1)), dma((steps, g - 1)),

time: 59.6 us -> 54.8 us (0.919)
  Pallas kernels: 55.9 us -> 51.1 us
    pallas_call x1, Pallas kernels: 55.9 us -> 51.1 us  [local(): pl.pallas_call(functools.partial(kernel, n, g, tdev, steps), out_shape=(o...]
where the time goes in v2:
time: 54.8 us; the launch traced here: 54.5 us
  Pallas kernels  51.1 us (93%)
  local copies, waits for them, and re-layouts  2.79 us (5%)
  between operations  0.64 us (1%)
    pallas_call x1, Pallas kernels, local(): pl.pallas_call(functools.partial(kernel, n, g, tdev, steps), out_shape=(o...  51.1 us
    unnamed x2, local copies, waits for them, and re-layouts  2.79 us

profile of v2, /device:TPU:0, one launch (start us, length us, event | category | flops | bytes accessed | tf_op | source)
XLA Modules:
  0.0 54.5 jit_solution(3697305407468493505)
XLA Ops:
  0.6 51.1 %shard_map.122 = (bf16[2,8192]{1,0:T(2,128)(2,1)}, bf16[2,8192]{1,0:T(2,128)(2,1)}) custom-call(s32[1,64]{1,0:T(1,128)} %bitcast.5, bf16[2,8192]{1,0:T(2,128)(2,1)} %in_ref.1, bf16[2,8192]{1,0:T(2,128)(2,1)} %q_ref.1, bf16[2,8192]{1,0:T(2,128)(2,1)} %k_ref.1, bf16[2,8192]{1,0:T(2,128)(2,1)} %v_ref.1, bf16[1536,4096]{1,0:T(8,128)(2,1)} %pk_hbm.1, ...), custom_call_target="tpu_custom_call" | custom-call | tf_op jit(solution)/shard_map/pallas_call | solution.py:430
  51.7 1.4 %copy.15 = bf16[2,8192]{1,0:T(2,128)(2,1)} copy(bf16[2,8192]{1,0:T(2,128)(2,1)} %get-tuple-element.4) | data formatting | bytes 65536
  53.1 1.4 %copy.16 = bf16[2,8192]{1,0:T(2,128)(2,1)} copy(bf16[2,8192]{1,0:T(2,128)(2,1)} %get-tuple-element.5) | data formatting | bytes 65536
